TPU v7x, 128 devices: a whole 4x4x4 slice. The times are simulated.
128 devices in a mesh: rows: 32 (over z, y, core), cols: 4 (over x).
Axes of the slice: x: 4, y: 4, z: 4, core: 2. Of those that a mesh axis runs over, the one named last changes fastest.
Arguments:
- basis: float32 [64, 262144], P('cols', 'rows'), may hold values from -450 to 450
- blocks: bfloat16 [1024, 4, 256, 256], P('rows'), may hold values from -16 to 1, as said below
- far_cols: int32 [1024], P('rows'), may hold values from 0 to 1023, as said below
Outputs:
- basis_out: float32 [64, 262144], P('cols', 'rows')
- ritz: float32 [64, 64], P(None, 'cols')
Inputs may be any that keep to these rules, and one draw needn't show every extreme that they name: Off-diagonal entries are positive; each diagonal entry of a diagonal block is minus the sum of the other entries of its row over the four blocks, rounded to bfloat16. `far_cols`: the block rows of one device name at most 2 far columns among the block rows of any one device; the block rows of some device are named by exactly 2 block rows of every device.
All inputs are finite; a program needn't handle non-finite values.
Results may differ from a plain program's by a relative error of at most 0.0036.
Values may be sent and summed in bfloat16 or wider, within the bound.
No kernel may reach another device: no remote copies, remote signals or barrier semaphores. Data moves between devices by JAX's collectives and lax.ppermute only.
A program may use at most 128 MiB of HBM per device.

v0:
```python
import jax
import jax.numpy as jnp
from jax import lax
from jax.sharding import PartitionSpec as P

ITERS = 4


def with_halo(block, sides, width):
    for axis, dim in sides:
        count = lax.axis_size(axis)
        forward = [(i, i + 1) for i in range(count - 1)]
        forward.append((count - 1, 0))
        backward = [(target, source) for source, target in forward]
        low = lax.ppermute(
            lax.slice_in_dim(block, block.shape[dim] - width, None, axis=dim), axis, forward
        )
        high = lax.ppermute(lax.slice_in_dim(block, 0, width, axis=dim), axis, backward)
        block = jnp.concatenate([low, block, high], axis=dim)
    return block


def block_product(pieces, blocks, position):
    return jnp.einsum(
        "jbt,bst->jbs", pieces, blocks[:, position], preferred_element_type=jnp.float32
    )


def body(basis, blocks, far_cols):
    width = basis.shape[0]
    block_rows = blocks.shape[0]
    block_size = blocks.shape[2]
    row_devices = lax.axis_size("rows")
    total_states = block_rows * block_size * row_devices
    modes = width * lax.axis_size("cols")
    highest = lax.Precision.HIGHEST

    def apply_generator(iterate_bf):
        shaped = iterate_bf.reshape(width, block_rows, block_size)
        result = block_product(shaped, blocks, 0)
        empty = jnp.zeros((width, block_rows, block_size), jnp.bfloat16)
        piece = lax.all_gather(shaped, "rows", axis=1, tiled=True)
        inside = jnp.logical_and(far_cols >= 0, far_cols < piece.shape[1])
        taken = jnp.take(piece, jnp.clip(far_cols, 0, piece.shape[1] - 1), axis=1)
        remote = jnp.where(inside[None, :, None], taken, empty)
        extended = with_halo(shaped, (("rows", 1),), 1)
        result = result + block_product(extended[:, :-2], blocks, 1)
        result = result + block_product(extended[:, 2:], blocks, 2)
        result = result + block_product(remote, blocks, 3)
        return result.reshape(width, block_rows * block_size)

    iterate = basis
    for step in range(ITERS):
        iterate = iterate + 0.2 * apply_generator(iterate.astype(jnp.bfloat16))
    whole_iterate = lax.all_gather(iterate, "cols", axis=0, tiled=True)
    contract = (((1,), (1,)), ((), ()))
    gram_part = lax.dot_general(whole_iterate, iterate, contract, precision=highest)
    column_start = lax.axis_index("cols") * width
    gram_mine = lax.psum(gram_part, "rows")
    gram = lax.all_gather(gram_mine, "cols", axis=1, tiled=True) / total_states
    applied = apply_generator(iterate.astype(jnp.bfloat16))
    product_part = lax.dot_general(whole_iterate, applied, contract, precision=highest)
    product_mine = lax.psum(product_part, "rows")
    product = lax.all_gather(product_mine, "cols", axis=1, tiled=True) / total_states
    factor = jnp.linalg.cholesky(gram)
    identity_square = jnp.eye(modes, dtype=factor.dtype)
    inverse_factor = lax.linalg.triangular_solve(
        factor, identity_square, left_side=True, lower=True
    )
    own_rows = lax.dynamic_slice_in_dim(inverse_factor, column_start, width, 0)
    basis_out = jnp.dot(own_rows, whole_iterate, precision=highest)
    left_part = jnp.dot(inverse_factor, product, precision=highest)
    ritz_whole = jnp.dot(left_part, inverse_factor.T, precision=highest)
    ritz = lax.dynamic_slice_in_dim(ritz_whole, column_start, width, 1)
    return (basis_out, ritz)


def solution(mesh):
    in_specs = (P("cols", "rows"), P("rows", None, None, None), P("rows"))
    out_specs = (P("cols", "rows"), P(None, "cols"))
    return jax.shard_map(body, mesh=mesh, in_specs=in_specs, out_specs=out_specs, check_vma=False)
```

profile of v0, /device:TPU:0, one launch (start us, length us, event | category | flops | bytes accessed | tf_op | source)
XLA Modules:
  0.0 539.1 jit_solution(13265493274930220181)
XLA Ops:
  7.2 1.1 convert_element_type.16
  9.8 6.0 %collective-permute-start.1 = (bf16[16,1,256]{2,0,1:T(8,128)(2,1)S(1)}, bf16[16,1,256]{2,0,1:T(8,128)(2,1)S(1)}, u32[]{:S(2)}, u32[]{:S(2)}) collective-permute-start(bf16[16,1,256]{2,0,1:T(8,128)(2,1)S(1)} %get-tuple-element.23), channel_id=1, source_target_pairs={{4,0},{8,4},{12,8},{16,12},{20,16},{24,20},{28,24},{32,28},{36,32}... | collective-permute-start | bytes 24584 | tf_op jit(solution)/shard_map/ppermute | solution.py:18
  16.5 3.4 fusion.60
  19.9 3.6 fusion.84
  23.5 3.5 fusion.81
  27.0 39.3 %all-gather.7.cloned.1.call-done = bf16[16,1024,256]{2,0,1:T(8,128)(2,1)} async-done(((bf16[16,32,256]{2,0,1:T(8,128)(2,1)}), bf16[16,1024,256]{2,0,1:T(8,128)(2,1)}) %all-gather.7.cloned.1.call-update) | async-done | bytes 8388624 | tf_op jit(solution)/shard_map/all_gather | solution.py:42
  66.4 3.9 gather_fusion
  70.3 3.4 fusion.72
  75.4 2.8 collective-permute-start.3
  78.2 3.4 fusion.36
  81.6 3.6 fusion.16
  85.2 42.1 %all-gather.9.cloned.1.call-done = bf16[16,1024,256]{2,0,1:T(8,128)(2,1)} async-done(((bf16[16,32,256]{2,0,1:T(8,128)(2,1)}), bf16[16,1024,256]{2,0,1:T(8,128)(2,1)}) %all-gather.9.cloned.1.call-update) | async-done | bytes 8388624 | tf_op jit(solution)/shard_map/all_gather | solution.py:42
  127.3 3.9 gather_fusion.1
  131.2 3.4 fusion.6
  134.7 3.4 fusion.141
  139.7 2.8 collective-permute-start.5
  142.5 3.4 fusion.34
  145.9 3.6 fusion.14
  149.6 42.1 %all-gather.11.cloned.1.call-done = bf16[16,1024,256]{2,0,1:T(8,128)(2,1)} async-done(((bf16[16,32,256]{2,0,1:T(8,128)(2,1)}), bf16[16,1024,256]{2,0,1:T(8,128)(2,1)}) %all-gather.11.cloned.1.call-update) | async-done | bytes 8388624 | tf_op jit(solution)/shard_map/all_gather | solution.py:42
  191.6 3.9 gather_fusion.2
  195.6 3.4 fusion.4
  199.0 3.4 fusion.129
  202.5 0.7 copy.155
  204.0 2.8 collective-permute-start.7
  206.9 3.4 fusion.32
  210.3 3.6 fusion.12
  213.9 42.1 %all-gather.13.cloned.1.call-done = bf16[16,1024,256]{2,0,1:T(8,128)(2,1)} async-done(((bf16[16,32,256]{2,0,1:T(8,128)(2,1)}), bf16[16,1024,256]{2,0,1:T(8,128)(2,1)}) %all-gather.13.cloned.1.call-update) | async-done | bytes 8388624 | tf_op jit(solution)/shard_map/all_gather | solution.py:42
  256.0 3.9 gather_fusion.3
  259.9 3.4 fusion.2
  263.3 3.4 fusion.117
  266.8 0.9 fusion.230
  267.7 0.7 copy.154
  269.2 2.8 collective-permute-start.9
  272.0 3.4 fusion.30
  275.5 3.8 fusion.10
  279.3 18.8 %all-gather.15.cloned.1.call-done = f32[64,8192]{1,0:T(8,128)} async-done(((f32[16,8192]{1,0:T(8,128)}), f32[64,8192]{1,0:T(8,128)}) %all-gather.15.cloned.1.call-update) | async-done | bytes 2097168 | tf_op jit(solution)/shard_map/all_gather | solution.py:55
  298.1 3.3 fusion.239
  301.5 51.9 %all-gather.17.cloned.1.call-done = bf16[16,1024,256]{2,0,1:T(8,128)(2,1)} async-done(((bf16[16,32,256]{2,0,1:T(8,128)(2,1)}), bf16[16,1024,256]{2,0,1:T(8,128)(2,1)}) %all-gather.17.cloned.1.call-update) | async-done | bytes 8388624 | tf_op jit(solution)/shard_map/all_gather | solution.py:42
  353.3 3.9 gather_fusion.4
  357.3 3.4 fusion
  360.7 3.6 fusion.105
  364.4 1.7 fusion.240
  366.1 126.6 %all-reduce = (f32[64,16]{0,1:T(8,128)S(1)}, f32[64,16]{0,1:T(8,128)S(1)}) all-reduce(f32[64,16]{0,1:T(8,128)S(1)} %fusion.239, f32[64,16]{0,1:T(8,128)S(1)} %fusion.240), channel_id=1, replica_groups=mesh['rows'=32,'cols'=4] {'rows'}, use_global_device_ids=true, to_apply=%region_0.2 | all-reduce | flops 2048 | bytes 16384 | tf_op jit(solution)/shard_map/psum | solution.py:59
  492.6 12.4 %all_gather.29 = f32[64,64]{0,1:T(8,128)S(1)} all-gather(f32[64,16]{0,1:T(8,128)S(1)} %get-tuple-element.3), channel_id=1, replica_groups=mesh['rows'=32,'cols'=4] {'cols'}, dimensions={1}, use_global_device_ids=true | all-gather | bytes 20480 | tf_op jit(solution)/shard_map/all_gather | solution.py:60
  505.2 5.8 %cholesky.17 = f32[64,64]{1,0:T(8,128)S(1)} custom-call(f32[64,64]{1,0:T(8,128)S(1)} %fusion.202), custom_call_target="Cholesky" | custom-call | tf_op jit(solution)/shard_map/jit(cholesky)/cholesky | solution.py:65
  512.4 4.9 custom-call.6
  517.5 11.9 %all_gather.31 = f32[64,64]{0,1:T(8,128)S(1)} all-gather(f32[64,16]{0,1:T(8,128)S(1)} %get-tuple-element.4), channel_id=1, replica_groups=mesh['rows'=32,'cols'=4] {'cols'}, dimensions={1}, use_global_device_ids=true | all-gather | bytes 20480 | tf_op jit(solution)/shard_map/all_gather | solution.py:64
  530.4 1.9 fusion.206
  (71 shorter events, 10.0 us)
Async XLA Ops:
  7.2 59.2 %all-gather.7.cloned.1.call-start = ((), (), s32[]{:S(2)}) async-start(), calls=%async_computation | async-start | bytes 8650752 | tf_op jit(solution)/shard_map/all_gather | solution.py:42
  9.0 118.3 %all-gather.9.cloned.1.call-start = ((), (), s32[]{:S(2)}) async-start(), calls=%async_computation.1 | async-start | bytes 8650752 | tf_op jit(solution)/shard_map/all_gather | solution.py:42
  9.8 10.1 %collective-permute-start = (bf16[16,1,256]{2,0,1:T(8,128)(2,1)S(1)}, bf16[16,1,256]{2,0,1:T(8,128)(2,1)S(1)}, u32[]{:S(2)}, u32[]{:S(2)}) collective-permute-start(bf16[16,1,256]{2,0,1:T(8,128)(2,1)S(1)} %get-tuple-element.24), channel_id=1, source_target_pairs={{0,4},{4,8},{8,12},{12,16},{16,20},{20,24},{24,28},{28,32},{32,36}... | collective-permute-start | bytes 24584 | tf_op jit(solution)/shard_map/ppermute | solution.py:15
  9.8 13.7 %collective-permute-start.1 = (bf16[16,1,256]{2,0,1:T(8,128)(2,1)S(1)}, bf16[16,1,256]{2,0,1:T(8,128)(2,1)S(1)}, u32[]{:S(2)}, u32[]{:S(2)}) collective-permute-start(bf16[16,1,256]{2,0,1:T(8,128)(2,1)S(1)} %get-tuple-element.23), channel_id=1, source_target_pairs={{4,0},{8,4},{12,8},{16,12},{20,16},{24,20},{28,24},{32,28},{36,32}... | collective-permute-start | bytes 24584 | tf_op jit(solution)/shard_map/ppermute | solution.py:18
  19.9 3.6 copy-start.4
  23.5 50.3 %copy-start.2 = (f32[16,8192]{1,0:T(8,128)S(1)}, f32[16,8192]{1,0:T(8,128)}, u32[]{:S(2)}) copy-start(f32[16,8192]{1,0:T(8,128)} %param.5) | copy-start | bytes 1572868
  74.6 117.0 %all-gather.11.cloned.1.call-start = ((), (), s32[]{:S(2)}) async-start(), calls=%async_computation.2 | async-start | bytes 8650752 | tf_op jit(solution)/shard_map/all_gather | solution.py:42
  75.4 6.2 %collective-permute-start.3 = (bf16[16,1,256]{2,0,1:T(8,128)(2,1)S(1)}, bf16[16,1,256]{2,0,1:T(8,128)(2,1)S(1)}, u32[]{:S(2)}, u32[]{:S(2)}) collective-permute-start(bf16[16,1,256]{2,0,1:T(8,128)(2,1)S(1)} %get-tuple-element.22), channel_id=1, source_target_pairs={{4,0},{8,4},{12,8},{16,12},{20,16},{24,20},{28,24},{32,28},{36,32}... | collective-permute-start | bytes 24584 | tf_op jit(solution)/shard_map/ppermute | solution.py:18
  81.6 53.1 %copy-start.5 = (bf16[2,32,8,256]{3,2,0,1:T(8,128)(2,1)S(1)}, bf16[2,32,8,256]{3,2,0,1:T(8,128)(2,1)}, u32[]{:S(2)}) copy-start(bf16[2,32,8,256]{3,2,0,1:T(8,128)(2,1)} %copy.157) | copy-start | bytes 786436
  81.6 53.1 %collective-permute-start.2 = (bf16[16,1,256]{2,0,1:T(8,128)(2,1)S(1)}, bf16[16,1,256]{2,0,1:T(8,128)(2,1)S(1)}, u32[]{:S(2)}, u32[]{:S(2)}) collective-permute-start(bf16[16,1,256]{2,0,1:T(8,128)(2,1)S(1)} %get-tuple-element.21), channel_id=1, source_target_pairs={{0,4},{4,8},{8,12},{12,16},{16,20},{20,24},{24,28},{28,32},{32,36}... | collective-permute-start | bytes 24584 | tf_op jit(solution)/shard_map/ppermute | solution.py:15
  138.9 117.0 %all-gather.13.cloned.1.call-start = ((), (), s32[]{:S(2)}) async-start(), calls=%async_computation.3 | async-start | bytes 8650752 | tf_op jit(solution)/shard_map/all_gather | solution.py:42
  139.7 6.2 %collective-permute-start.5 = (bf16[16,1,256]{2,0,1:T(8,128)(2,1)S(1)}, bf16[16,1,256]{2,0,1:T(8,128)(2,1)S(1)}, u32[]{:S(2)}, u32[]{:S(2)}) collective-permute-start(bf16[16,1,256]{2,0,1:T(8,128)(2,1)S(1)} %get-tuple-element.20), channel_id=1, source_target_pairs={{4,0},{8,4},{12,8},{16,12},{20,16},{24,20},{28,24},{32,28},{36,32}... | collective-permute-start | bytes 24584 | tf_op jit(solution)/shard_map/ppermute | solution.py:18
  145.9 53.1 %copy-start.6 = (bf16[2,32,8,256]{3,2,0,1:T(8,128)(2,1)S(1)}, bf16[2,32,8,256]{3,2,0,1:T(8,128)(2,1)}, u32[]{:S(2)}) copy-start(bf16[2,32,8,256]{3,2,0,1:T(8,128)(2,1)} %copy.156) | copy-start | bytes 786436
  145.9 53.1 %collective-permute-start.4 = (bf16[16,1,256]{2,0,1:T(8,128)(2,1)S(1)}, bf16[16,1,256]{2,0,1:T(8,128)(2,1)S(1)}, u32[]{:S(2)}, u32[]{:S(2)}) collective-permute-start(bf16[16,1,256]{2,0,1:T(8,128)(2,1)S(1)} %get-tuple-element.19), channel_id=1, source_target_pairs={{0,4},{4,8},{8,12},{12,16},{16,20},{20,24},{24,28},{28,32},{32,36}... | collective-permute-start | bytes 24584 | tf_op jit(solution)/shard_map/ppermute | solution.py:15
  203.3 94.9 %all-gather.15.cloned.1.call-start = ((), (), s32[]{:S(2)}) async-start(), calls=%async_computation.4 | async-start | bytes 2621440 | tf_op jit(solution)/shard_map/all_gather | solution.py:55
  204.0 6.2 %collective-permute-start.7 = (bf16[16,1,256]{2,0,1:T(8,128)(2,1)S(1)}, bf16[16,1,256]{2,0,1:T(8,128)(2,1)S(1)}, u32[]{:S(2)}, u32[]{:S(2)}) collective-permute-start(bf16[16,1,256]{2,0,1:T(8,128)(2,1)S(1)} %get-tuple-element.18), channel_id=1, source_target_pairs={{4,0},{8,4},{12,8},{16,12},{20,16},{24,20},{28,24},{32,28},{36,32}... | collective-permute-start | bytes 24584 | tf_op jit(solution)/shard_map/ppermute | solution.py:18
  210.3 53.1 %copy-start.7 = (bf16[2,32,8,256]{3,2,0,1:T(8,128)(2,1)S(1)}, bf16[2,32,8,256]{3,2,0,1:T(8,128)(2,1)}, u32[]{:S(2)}) copy-start(bf16[2,32,8,256]{3,2,0,1:T(8,128)(2,1)} %copy.155) | copy-start | bytes 786436
  210.3 53.1 %collective-permute-start.6 = (bf16[16,1,256]{2,0,1:T(8,128)(2,1)S(1)}, bf16[16,1,256]{2,0,1:T(8,128)(2,1)S(1)}, u32[]{:S(2)}, u32[]{:S(2)}) collective-permute-start(bf16[16,1,256]{2,0,1:T(8,128)(2,1)S(1)} %get-tuple-element.17), channel_id=1, source_target_pairs={{0,4},{4,8},{8,12},{12,16},{16,20},{20,24},{24,28},{28,32},{32,36}... | collective-permute-start | bytes 24584 | tf_op jit(solution)/shard_map/ppermute | solution.py:15
  267.7 85.7 %all-gather.17.cloned.1.call-start = ((), (), s32[]{:S(2)}) async-start(), calls=%async_computation.5 | async-start | bytes 8650752 | tf_op jit(solution)/shard_map/all_gather | solution.py:42
  269.2 6.2 %collective-permute-start.9 = (bf16[16,1,256]{2,0,1:T(8,128)(2,1)S(1)}, bf16[16,1,256]{2,0,1:T(8,128)(2,1)S(1)}, u32[]{:S(2)}, u32[]{:S(2)}) collective-permute-start(bf16[16,1,256]{2,0,1:T(8,128)(2,1)S(1)} %get-tuple-element.16), channel_id=1, source_target_pairs={{4,0},{8,4},{12,8},{16,12},{20,16},{24,20},{28,24},{32,28},{36,32}... | collective-permute-start | bytes 24584 | tf_op jit(solution)/shard_map/ppermute | solution.py:18
  275.4 22.7 %copy-start.1 = (f32[16,8192]{1,0:T(8,128)S(1)}, f32[16,8192]{1,0:T(8,128)}, u32[]{:S(2)}) copy-start(f32[16,8192]{1,0:T(8,128)} %get-tuple-element.6) | copy-start | bytes 1572868
  275.4 85.3 %copy-start.3 = (bf16[2,32,8,256]{3,2,0,1:T(8,128)(2,1)S(1)}, bf16[2,32,8,256]{3,2,0,1:T(8,128)(2,1)}, u32[]{:S(2)}) copy-start(bf16[2,32,8,256]{3,2,0,1:T(8,128)(2,1)} %copy.154) | copy-start | bytes 786436
  275.4 85.3 %collective-permute-start.8 = (bf16[16,1,256]{2,0,1:T(8,128)(2,1)S(1)}, bf16[16,1,256]{2,0,1:T(8,128)(2,1)S(1)}, u32[]{:S(2)}, u32[]{:S(2)}) collective-permute-start(bf16[16,1,256]{2,0,1:T(8,128)(2,1)S(1)} %get-tuple-element.15), channel_id=1, source_target_pairs={{0,4},{4,8},{8,12},{12,16},{16,20},{20,24},{24,28},{28,32},{32,36}... | collective-permute-start | bytes 24584 | tf_op jit(solution)/shard_map/ppermute | solution.py:15
  360.7 3.6 copy-start
Sparse Core Ops, SparseCore 0:
  10.8 55.4 all-gather.6
  74.7 52.5 all-gather.8
  139.1 52.5 all-gather.10
  203.4 52.5 all-gather.12
  267.8 30.2 all-gather.14
  300.2 53.0 all-gather.16
where the time goes:
time: 540 us; the launch traced here: 539 us
  waiting for transfers between devices  236 us (44%)
  blocking collectives  151 us (28%)
  matrix products  77.1 us (14%)
  local copies, waits for them, and re-layouts  27.9 us (5%)
  starting transfers between devices  17.6 us (3%)
  other arithmetic  14.9 us (3%)
  between operations  14.4 us (3%)
    all_gather x5, waiting for transfers between devices, apply_generator(): piece = lax.all_gather(shaped, 'rows', axis=1, tiled=True)  217 us
    psum x1, blocking collectives, body(): gram_mine = lax.psum(gram_part, 'rows')  127 us
    dot_general x20, matrix products, block_product(): jnp.einsum('jbt,bst->jbs', pieces, blocks[:, position], preferred_element...  69.5 us
    gather x5, local copies, waits for them, and re-layouts, apply_generator(): taken = jnp.take(piece, jnp.clip(far_cols, 0, piece.shape[1] - 1), axis=1)  19.7 us
    all_gather x1, waiting for transfers between devices, body(): whole_iterate = lax.all_gather(iterate, 'cols', axis=0, tiled=True)  18.8 us
    ppermute x5, starting transfers between devices, with_halo(): lax.ppermute(lax.slice_in_dim(block, 0, width, axis=dim), axis, backward)  17.3 us
    all_gather x1, blocking collectives, body(): gram = lax.all_gather(gram_mine, 'cols', axis=1, tiled=True) / total_states  12.4 us
    all_gather x1, blocking collectives, body(): lax.all_gather(product_mine, 'cols', axis=1, tiled=True) / total_states  11.9 us
  transfers between devices with their start and end apart: 16, of which 6 were waited for; matrix products, arithmetic and copies ran while one was open for 14% of the time, Pallas kernels for 0%

commit v1 on v0

--- a/solution.py
+++ b/solution.py
@@ -56,7 +56,10 @@
     contract = (((1,), (1,)), ((), ()))
     gram_part = lax.dot_general(whole_iterate, iterate, contract, precision=highest)
     column_start = lax.axis_index("cols") * width
-    gram_mine = lax.psum(gram_part, "rows")
+    devices, gram_mine = (lax.axis_size("rows"), gram_part)
+    for stride in [1 << k for k in range(devices.bit_length() - 1)]:
+        route = [(i_2, i_2 ^ stride) for i_2 in range(devices)]
+        gram_mine = gram_mine + lax.ppermute(gram_mine, "rows", route)
     gram = lax.all_gather(gram_mine, "cols", axis=1, tiled=True) / total_states
     applied = apply_generator(iterate.astype(jnp.bfloat16))
     product_part = lax.dot_general(whole_iterate, applied, contract, precision=highest)

time: 540 us -> 454 us (0.84)
  blocking collectives: 151 us -> 91 us
  waiting for transfers between devices: 236 us -> 202 us
  starting transfers between devices: 17.6 us -> 25.1 us
    psum x1, blocking collectives: 127 us -> 66.5 us  [body(): product_mine = lax.psum(product_part, 'rows')]
    all_gather x5, waiting for transfers between devices: 217 us -> 168 us  [apply_generator(): piece = lax.all_gather(shaped, 'rows', axis=1, tiled=True)]
    all_gather x1, waiting for transfers between devices: 18.8 us -> 29.7 us  [body(): whole_iterate = lax.all_gather(iterate, 'cols', axis=0, tiled=True)]
    ppermute x0 -> x5, starting transfers between devices: none -> 8.52 us  [body(): gram_mine = gram_mine + lax.ppermute(gram_mine, 'rows', route)]
  transfers between devices with their start and end apart: 16 -> 21, of which waited for: 6 -> 8; matrix products, arithmetic and copies ran while one was open for 14% -> 20% of each run, Pallas kernels for 0% -> 0%
where the time goes in v1:
time: 454 us; the launch traced here: 453 us
  waiting for transfers between devices  202 us (44%)
  blocking collectives  91 us (20%)
  matrix products  77.7 us (17%)
  local copies, waits for them, and re-layouts  27.9 us (6%)
  starting transfers between devices  25.1 us (6%)
  other arithmetic  14.9 us (3%)
  between operations  14.5 us (3%)
    all_gather x5, waiting for transfers between devices, apply_generator(): piece = lax.all_gather(shaped, 'rows', axis=1, tiled=True)  168 us
    dot_general x20, matrix products, block_product(): jnp.einsum('jbt,bst->jbs', pieces, blocks[:, position], preferred_element...  70 us
    psum x1, blocking collectives, body(): product_mine = lax.psum(product_part, 'rows')  66.5 us
    all_gather x1, waiting for transfers between devices, body(): whole_iterate = lax.all_gather(iterate, 'cols', axis=0, tiled=True)  29.7 us
    gather x5, local copies, waits for them, and re-layouts, apply_generator(): taken = jnp.take(piece, jnp.clip(far_cols, 0, piece.shape[1] - 1), axis=1)  19.7 us
    ppermute x5, starting transfers between devices, with_halo(): lax.ppermute(lax.slice_in_dim(block, 0, width, axis=dim), axis, backward)  16.3 us
    all_gather x1, blocking collectives, body(): lax.all_gather(product_mine, 'cols', axis=1, tiled=True) / total_states  12.3 us
    all_gather x1, blocking collectives, body(): gram = lax.all_gather(gram_mine, 'cols', axis=1, tiled=True) / total_states  12.3 us
  transfers between devices with their start and end apart: 21, of which 8 were waited for; matrix products, arithmetic and copies ran while one was open for 20% of the time, Pallas kernels for 0%

profile of v1, /device:TPU:0, one launch (start us, length us, event | category | flops | bytes accessed | tf_op | source)
XLA Modules:
  0.0 452.6 jit_solution(7255846742896969997)
XLA Ops:
  9.8 6.0 %collective-permute-start.1 = (bf16[16,1,256]{2,0,1:T(8,128)(2,1)S(1)}, bf16[16,1,256]{2,0,1:T(8,128)(2,1)S(1)}, u32[]{:S(2)}, u32[]{:S(2)}) collective-permute-start(bf16[16,1,256]{2,0,1:T(8,128)(2,1)S(1)} %get-tuple-element.21), channel_id=1, source_target_pairs={{4,0},{8,4},{12,8},{16,12},{20,16},{24,20},{28,24},{32,28},{36,32}... | collective-permute-start | bytes 24584 | tf_op jit(solution)/shard_map/ppermute | solution.py:18
  16.5 3.4 fusion.60
  19.9 3.6 fusion.84
  23.5 3.5 fusion.81
  27.0 39.3 %all-gather.7.cloned.1.call-done = bf16[16,1024,256]{2,0,1:T(8,128)(2,1)} async-done(((bf16[16,32,256]{2,0,1:T(8,128)(2,1)}), bf16[16,1024,256]{2,0,1:T(8,128)(2,1)}) %all-gather.7.cloned.1.call-update) | async-done | bytes 8388624 | tf_op jit(solution)/shard_map/all_gather | solution.py:42
  66.4 3.9 gather_fusion
  70.3 3.4 fusion.72
  75.4 2.8 collective-permute-start.3
  78.2 3.4 fusion.36
  81.6 3.6 fusion.16
  85.2 42.1 %all-gather.9.cloned.1.call-done = bf16[16,1024,256]{2,0,1:T(8,128)(2,1)} async-done(((bf16[16,32,256]{2,0,1:T(8,128)(2,1)}), bf16[16,1024,256]{2,0,1:T(8,128)(2,1)}) %all-gather.9.cloned.1.call-update) | async-done | bytes 8388624 | tf_op jit(solution)/shard_map/all_gather | solution.py:42
  127.3 3.9 gather_fusion.1
  131.2 3.4 fusion.6
  134.7 3.4 fusion.141
  139.7 2.8 collective-permute-start.5
  142.5 3.4 fusion.34
  145.9 3.6 fusion.14
  149.6 42.1 %all-gather.11.cloned.1.call-done = bf16[16,1024,256]{2,0,1:T(8,128)(2,1)} async-done(((bf16[16,32,256]{2,0,1:T(8,128)(2,1)}), bf16[16,1024,256]{2,0,1:T(8,128)(2,1)}) %all-gather.11.cloned.1.call-update) | async-done | bytes 8388624 | tf_op jit(solution)/shard_map/all_gather | solution.py:42
  191.6 3.9 gather_fusion.2
  195.6 3.4 fusion.4
  199.0 3.4 fusion.129
  204.0 2.8 collective-permute-start.7
  206.9 3.4 fusion.32
  210.3 3.6 fusion.12
  213.9 42.1 %all-gather.13.cloned.1.call-done = bf16[16,1024,256]{2,0,1:T(8,128)(2,1)} async-done(((bf16[16,32,256]{2,0,1:T(8,128)(2,1)}), bf16[16,1024,256]{2,0,1:T(8,128)(2,1)}) %all-gather.13.cloned.1.call-update) | async-done | bytes 8388624 | tf_op jit(solution)/shard_map/all_gather | solution.py:42
  256.0 3.9 gather_fusion.3
  259.9 3.4 fusion.2
  263.3 3.4 fusion.117
  268.5 29.7 %all-gather.15.cloned.1.call-done = f32[64,8192]{1,0:T(8,128)} async-done(((f32[16,8192]{1,0:T(8,128)}), f32[64,8192]{1,0:T(8,128)}) %all-gather.15.cloned.1.call-update) | async-done | bytes 2097168 | tf_op jit(solution)/shard_map/all_gather | solution.py:55
  298.1 3.4 fusion.239
  302.7 1.5 collective-permute-start.9
  304.2 2.2 collective-permute-done.9
  306.4 3.0 collective-permute-start.10
  310.1 1.9 collective-permute-start.14
  313.1 3.4 fusion.30
  316.5 2.9 collective-permute-start.12
  319.4 4.4 fusion.10
  323.8 12.3 %all_gather.29 = f32[64,64]{0,1:T(8,128)S(1)} all-gather(f32[64,16]{0,1:T(8,128)S(1)} %add.129), channel_id=1, replica_groups=mesh['rows'=32,'cols'=4] {'cols'}, dimensions={1}, use_global_device_ids=true | all-gather | bytes 20480 | tf_op jit(solution)/shard_map/all_gather | solution.py:63
  336.2 5.8 %cholesky.17 = f32[64,64]{1,0:T(8,128)S(1)} custom-call(f32[64,64]{1,0:T(8,128)S(1)} %fusion.202), custom_call_target="Cholesky" | custom-call | tf_op jit(solution)/shard_map/jit(cholesky)/cholesky | solution.py:68
  343.4 4.9 %custom-call.6 = f32[1,64,64]{1,2,0:T(8,128)S(1)} custom-call(f32[1,64,64]{2,1,0:T(8,128)S(1)} %fusion.199), custom_call_target="InvertDiagBlocksLowerTriangular" | custom-call | tf_op jit(solution)/shard_map/triangular_solve | solution.py:70
  348.5 1.9 fusion.206
  350.4 2.9 all-gather.17.cloned.1.call-done
  353.3 3.9 gather_fusion.4
  357.3 3.4 fusion
  360.7 3.5 fusion.105
  364.3 1.7 fusion.240
  366.0 66.5 %psum.7 = f32[64,16]{0,1:T(8,128)S(1)} all-reduce(f32[64,16]{0,1:T(8,128)S(1)} %fusion.240), channel_id=1, replica_groups=mesh['rows'=32,'cols'=4] {'rows'}, use_global_device_ids=true, to_apply=%region_2.4 | all-reduce | flops 1024 | bytes 8192 | tf_op jit(solution)/shard_map/psum | solution.py:66
  432.5 12.3 %all_gather.31 = f32[64,64]{0,1:T(8,128)S(1)} all-gather(f32[64,16]{0,1:T(8,128)S(1)} %psum.7), channel_id=1, replica_groups=mesh['rows'=32,'cols'=4] {'cols'}, dimensions={1}, use_global_device_ids=true | all-gather | bytes 20480 | tf_op jit(solution)/shard_map/all_gather | solution.py:67
  (84 shorter events, 15.6 us)
Async XLA Ops:
  7.2 59.2 %all-gather.7.cloned.1.call-start = ((), (), s32[]{:S(2)}) async-start(), calls=%async_computation | async-start | bytes 8650752 | tf_op jit(solution)/shard_map/all_gather | solution.py:42
  9.0 118.3 %all-gather.9.cloned.1.call-start = ((), (), s32[]{:S(2)}) async-start(), calls=%async_computation.1 | async-start | bytes 8650752 | tf_op jit(solution)/shard_map/all_gather | solution.py:42
  9.8 10.1 %collective-permute-start = (bf16[16,1,256]{2,0,1:T(8,128)(2,1)S(1)}, bf16[16,1,256]{2,0,1:T(8,128)(2,1)S(1)}, u32[]{:S(2)}, u32[]{:S(2)}) collective-permute-start(bf16[16,1,256]{2,0,1:T(8,128)(2,1)S(1)} %get-tuple-element.22), channel_id=1, source_target_pairs={{0,4},{4,8},{8,12},{12,16},{16,20},{20,24},{24,28},{28,32},{32,36}... | collective-permute-start | bytes 24584 | tf_op jit(solution)/shard_map/ppermute | solution.py:15
  9.8 13.7 %collective-permute-start.1 = (bf16[16,1,256]{2,0,1:T(8,128)(2,1)S(1)}, bf16[16,1,256]{2,0,1:T(8,128)(2,1)S(1)}, u32[]{:S(2)}, u32[]{:S(2)}) collective-permute-start(bf16[16,1,256]{2,0,1:T(8,128)(2,1)S(1)} %get-tuple-element.21), channel_id=1, source_target_pairs={{4,0},{8,4},{12,8},{16,12},{20,16},{24,20},{28,24},{32,28},{36,32}... | collective-permute-start | bytes 24584 | tf_op jit(solution)/shard_map/ppermute | solution.py:18
  19.9 3.6 copy-start.3
  23.5 50.3 %copy-start.1 = (f32[16,8192]{1,0:T(8,128)S(1)}, f32[16,8192]{1,0:T(8,128)}, u32[]{:S(2)}) copy-start(f32[16,8192]{1,0:T(8,128)} %param.5) | copy-start | bytes 1572868
  74.6 117.0 %all-gather.11.cloned.1.call-start = ((), (), s32[]{:S(2)}) async-start(), calls=%async_computation.2 | async-start | bytes 8650752 | tf_op jit(solution)/shard_map/all_gather | solution.py:42
  75.4 6.2 %collective-permute-start.3 = (bf16[16,1,256]{2,0,1:T(8,128)(2,1)S(1)}, bf16[16,1,256]{2,0,1:T(8,128)(2,1)S(1)}, u32[]{:S(2)}, u32[]{:S(2)}) collective-permute-start(bf16[16,1,256]{2,0,1:T(8,128)(2,1)S(1)} %get-tuple-element.20), channel_id=1, source_target_pairs={{4,0},{8,4},{12,8},{16,12},{20,16},{24,20},{28,24},{32,28},{36,32}... | collective-permute-start | bytes 24584 | tf_op jit(solution)/shard_map/ppermute | solution.py:18
  81.6 53.1 %copy-start.4 = (bf16[2,32,8,256]{3,2,0,1:T(8,128)(2,1)S(1)}, bf16[2,32,8,256]{3,2,0,1:T(8,128)(2,1)}, u32[]{:S(2)}) copy-start(bf16[2,32,8,256]{3,2,0,1:T(8,128)(2,1)} %copy.157) | copy-start | bytes 786436
  81.6 53.1 %collective-permute-start.2 = (bf16[16,1,256]{2,0,1:T(8,128)(2,1)S(1)}, bf16[16,1,256]{2,0,1:T(8,128)(2,1)S(1)}, u32[]{:S(2)}, u32[]{:S(2)}) collective-permute-start(bf16[16,1,256]{2,0,1:T(8,128)(2,1)S(1)} %get-tuple-element.19), channel_id=1, source_target_pairs={{0,4},{4,8},{8,12},{12,16},{16,20},{20,24},{24,28},{28,32},{32,36}... | collective-permute-start | bytes 24584 | tf_op jit(solution)/shard_map/ppermute | solution.py:15
  138.9 117.0 %all-gather.13.cloned.1.call-start = ((), (), s32[]{:S(2)}) async-start(), calls=%async_computation.3 | async-start | bytes 8650752 | tf_op jit(solution)/shard_map/all_gather | solution.py:42
  139.7 6.2 %collective-permute-start.5 = (bf16[16,1,256]{2,0,1:T(8,128)(2,1)S(1)}, bf16[16,1,256]{2,0,1:T(8,128)(2,1)S(1)}, u32[]{:S(2)}, u32[]{:S(2)}) collective-permute-start(bf16[16,1,256]{2,0,1:T(8,128)(2,1)S(1)} %get-tuple-element.18), channel_id=1, source_target_pairs={{4,0},{8,4},{12,8},{16,12},{20,16},{24,20},{28,24},{32,28},{36,32}... | collective-permute-start | bytes 24584 | tf_op jit(solution)/shard_map/ppermute | solution.py:18
  145.9 53.1 %copy-start.5 = (bf16[2,32,8,256]{3,2,0,1:T(8,128)(2,1)S(1)}, bf16[2,32,8,256]{3,2,0,1:T(8,128)(2,1)}, u32[]{:S(2)}) copy-start(bf16[2,32,8,256]{3,2,0,1:T(8,128)(2,1)} %copy.156) | copy-start | bytes 786436
  145.9 53.1 %collective-permute-start.4 = (bf16[16,1,256]{2,0,1:T(8,128)(2,1)S(1)}, bf16[16,1,256]{2,0,1:T(8,128)(2,1)S(1)}, u32[]{:S(2)}, u32[]{:S(2)}) collective-permute-start(bf16[16,1,256]{2,0,1:T(8,128)(2,1)S(1)} %get-tuple-element.17), channel_id=1, source_target_pairs={{0,4},{4,8},{8,12},{12,16},{16,20},{20,24},{24,28},{28,32},{32,36}... | collective-permute-start | bytes 24584 | tf_op jit(solution)/shard_map/ppermute | solution.py:15
  203.3 94.9 %all-gather.15.cloned.1.call-start = ((), (), s32[]{:S(2)}) async-start(), calls=%async_computation.4 | async-start | bytes 2621440 | tf_op jit(solution)/shard_map/all_gather | solution.py:55
  204.0 6.2 %collective-permute-start.7 = (bf16[16,1,256]{2,0,1:T(8,128)(2,1)S(1)}, bf16[16,1,256]{2,0,1:T(8,128)(2,1)S(1)}, u32[]{:S(2)}, u32[]{:S(2)}) collective-permute-start(bf16[16,1,256]{2,0,1:T(8,128)(2,1)S(1)} %get-tuple-element.16), channel_id=1, source_target_pairs={{4,0},{8,4},{12,8},{16,12},{20,16},{24,20},{28,24},{32,28},{36,32}... | collective-permute-start | bytes 24584 | tf_op jit(solution)/shard_map/ppermute | solution.py:18
  210.3 53.1 %copy-start.6 = (bf16[2,32,8,256]{3,2,0,1:T(8,128)(2,1)S(1)}, bf16[2,32,8,256]{3,2,0,1:T(8,128)(2,1)}, u32[]{:S(2)}) copy-start(bf16[2,32,8,256]{3,2,0,1:T(8,128)(2,1)} %copy.155) | copy-start | bytes 786436
  210.3 53.1 %collective-permute-start.6 = (bf16[16,1,256]{2,0,1:T(8,128)(2,1)S(1)}, bf16[16,1,256]{2,0,1:T(8,128)(2,1)S(1)}, u32[]{:S(2)}, u32[]{:S(2)}) collective-permute-start(bf16[16,1,256]{2,0,1:T(8,128)(2,1)S(1)} %get-tuple-element.15), channel_id=1, source_target_pairs={{0,4},{4,8},{8,12},{12,16},{16,20},{20,24},{24,28},{28,32},{32,36}... | collective-permute-start | bytes 24584 | tf_op jit(solution)/shard_map/ppermute | solution.py:15
  267.7 85.7 %all-gather.17.cloned.1.call-start = ((), (), s32[]{:S(2)}) async-start(), calls=%async_computation.5 | async-start | bytes 8650752 | tf_op jit(solution)/shard_map/all_gather | solution.py:42
  301.5 1.2 collective-permute-start.8
  302.7 3.7 collective-permute-start.9
  306.4 5.6 %collective-permute-start.10 = (f32[64,16]{0,1:T(8,128)S(1)}, f32[64,16]{0,1:T(8,128)S(1)}, u32[]{:S(2)}, u32[]{:S(2)}) collective-permute-start(f32[64,16]{0,1:T(8,128)S(1)} %add.126), channel_id=1, source_target_pairs={{0,16},{4,20},{8,24},{12,28},{16,0},{20,4},{24,8},{28,12},{32,48},... | collective-permute-start | bytes 12296 | tf_op jit(solution)/shard_map/ppermute | solution.py:62
  310.1 9.3 %collective-permute-start.14 = (bf16[16,1,256]{2,0,1:T(8,128)(2,1)S(1)}, bf16[16,1,256]{2,0,1:T(8,128)(2,1)S(1)}, u32[]{:S(2)}, u32[]{:S(2)}) collective-permute-start(bf16[16,1,256]{2,0,1:T(8,128)(2,1)S(1)} %get-tuple-element.14), channel_id=1, source_target_pairs={{4,0},{8,4},{12,8},{16,12},{20,16},{24,20},{28,24},{32,28},{36,32}... | collective-permute-start | bytes 24584 | tf_op jit(solution)/shard_map/ppermute | solution.py:18
  312.0 4.5 collective-permute-start.11
  316.5 44.2 %collective-permute-start.13 = (bf16[16,1,256]{2,0,1:T(8,128)(2,1)S(1)}, bf16[16,1,256]{2,0,1:T(8,128)(2,1)S(1)}, u32[]{:S(2)}, u32[]{:S(2)}) collective-permute-start(bf16[16,1,256]{2,0,1:T(8,128)(2,1)S(1)} %get-tuple-element.13), channel_id=1, source_target_pairs={{0,4},{4,8},{8,12},{12,16},{16,20},{20,24},{24,28},{28,32},{32,36}... | collective-permute-start | bytes 24584 | tf_op jit(solution)/shard_map/ppermute | solution.py:15
  316.5 32.0 %copy-start = (f32[64,8192]{1,0:T(8,128)S(1)}, f32[64,8192]{1,0:T(8,128)}, u32[]{:S(2)}) copy-start(f32[64,8192]{1,0:T(8,128)} %all-gather.15.cloned.1.call-done) | copy-start | bytes 6291460
  316.5 7.3 %collective-permute-start.12 = (f32[64,16]{0,1:T(8,128)S(1)}, f32[64,16]{0,1:T(8,128)S(1)}, u32[]{:S(2)}, u32[]{:S(2)}) collective-permute-start(f32[64,16]{0,1:T(8,128)S(1)} %add.128), channel_id=1, source_target_pairs={{0,64},{4,68},{8,72},{12,76},{16,80},{20,84},{24,88},{28,92},{32,9... | collective-permute-start | bytes 12296 | tf_op jit(solution)/shard_map/ppermute | solution.py:62
  323.8 36.9 %copy-start.2 = (bf16[2,32,8,256]{3,2,0,1:T(8,128)(2,1)S(1)}, bf16[2,32,8,256]{3,2,0,1:T(8,128)(2,1)}, u32[]{:S(2)}) copy-start(bf16[2,32,8,256]{3,2,0,1:T(8,128)(2,1)} %copy.154) | copy-start | bytes 786436
Sparse Core Ops, SparseCore 0:
  10.8 55.4 all-gather.6
  74.7 52.5 all-gather.8
  139.1 52.5 all-gather.10
  203.4 52.5 all-gather.12
  267.8 30.2 all-gather.14
  300.2 53.0 all-gather.16
